TPU v7x, 128 devices: a whole 4x4x4 slice. The times are simulated.
128 devices in a mesh: dp: 64 (over y, z, x), mp: 2 (over core).
Axes of the slice: x: 4, y: 4, z: 4, core: 2. Of those that a mesh axis runs over, the one named last changes fastest.
Arguments:
- grads: bfloat16 [16384, 6144], P('dp', 'mp'), may hold values from -0.796875 to 0.796875
- slot_block: int32 [128], replicated, may hold values from -1 to 95, as said below
- left_stats: float32 [128, 1024, 1024], P('dp', 'mp'), may hold values from -6 to 6
- right_stats: float32 [128, 1024, 1024], P('dp', 'mp'), may hold values from -6 to 6
- left_root: bfloat16 [128, 1024, 1024], P('dp', 'mp'), may hold values from -0.59765625 to 0.59765625
- right_root: bfloat16 [128, 1024, 1024], P('dp', None, 'mp'), may hold values from -0.59765625 to 0.59765625
Outputs:
- direction: bfloat16 [16384, 6144], P('dp', 'mp')
- new_left: float32 [128, 1024, 1024], P('dp', 'mp')
- new_right: float32 [128, 1024, 1024], P('dp', 'mp')
Inputs may be any that keep to these rules, and one draw needn't show every extreme that they name: slot_block[s] names the block whose statistics sit in slot s, or -1 for an empty slot; every block 0 to 95 stands in exactly one slot; slots k * 2 to k * 2 + 1 lie on dp index k, and some dp index holds 2 blocks.
All inputs are finite; a program needn't handle non-finite values.
Results may differ from a plain program's by a relative error of at most 0.005.
Values may be sent and summed in bfloat16 or wider, within the bound.
A program may use at most 128 MiB of HBM per device.

v0:
```python
import jax
import jax.numpy as jnp
from jax import lax
from jax.sharding import PartitionSpec as P

beta_decay = 0.9


def partner(value, axis, stride):
    mask = 2**stride
    pairs = [(source, source ^ mask) for source in range(lax.axis_size(axis))]
    return lax.ppermute(value, axis, pairs)


def on_device(grads, slot_block, left_stats, right_stats, left_root, right_root):
    dp_count = lax.axis_size("dp")
    capacity = left_stats.shape[0]
    half_width = left_stats.shape[1]
    block_width = left_stats.shape[2]
    local_rows = grads.shape[0]
    local_cols = grads.shape[1]
    per_core = local_cols // block_width
    block_cols = 2 * per_core
    group_rows = local_rows * dp_count // block_width
    quarter = block_width // local_rows
    sliver = local_rows // dp_count
    piece_rows = quarter * sliver
    core_index = lax.axis_index("mp")
    banded = lax.all_to_all(grads, "dp", split_axis=0, concat_axis=0, tiled=True)
    tiles = banded.reshape(group_rows, quarter, sliver, per_core, block_width)
    tiles = tiles.transpose(0, 3, 1, 2, 4).reshape(group_rows * per_core, piece_rows, block_width)
    slot_table = slot_block.reshape(dp_count, capacity).T
    filled = slot_table >= 0
    safe_ids = jnp.maximum(slot_table, 0)
    block_row = safe_ids // block_cols
    block_col = safe_ids % block_cols
    mine = jnp.logical_and(filled, block_col // per_core == core_index)
    tile_ids = block_row * per_core + block_col % per_core
    picked = tiles[tile_ids]
    picked = jnp.where(mine[:, :, None, None], picked, jnp.zeros_like(picked))
    doubled = jnp.broadcast_to(picked[:, :, None], (capacity, dp_count, 2, piece_rows, block_width))
    doubled = doubled.reshape(capacity, dp_count * 2 * piece_rows, block_width)
    arrived = lax.all_to_all(doubled, ("dp", "mp"), split_axis=1, concat_axis=1, tiled=True)
    arrived = arrived.reshape(capacity, dp_count, 2, quarter, sliver, block_width)
    merged = arrived[:, :, 0] + arrived[:, :, 1]
    full_block = merged.transpose(0, 2, 1, 3, 4).reshape(capacity, block_width, block_width)
    own_rows = lax.dynamic_slice_in_dim(full_block, core_index * half_width, half_width, 1)
    own_cols = lax.dynamic_slice_in_dim(full_block, core_index * half_width, half_width, 2)
    gram_left = jnp.einsum("crk,csk->crs", own_rows, full_block, preferred_element_type=jnp.float32)
    gram_right = jnp.einsum(
        "ckr,cks->crs", own_cols, full_block, preferred_element_type=jnp.float32
    )
    new_left = beta_decay * left_stats + (1.0 - beta_decay) * gram_left
    new_right = beta_decay * right_stats + (1.0 - beta_decay) * gram_right
    left_part = jnp.einsum(
        "crk,cks->crs", left_root, full_block, preferred_element_type=jnp.float32
    ).astype(jnp.bfloat16)
    other_part = partner(left_part, "mp", 0)
    upper_half = jnp.where(core_index == 0, left_part, other_part)
    lower_half = jnp.where(core_index == 0, other_part, left_part)
    full_left = jnp.concatenate([upper_half, lower_half], axis=1)
    dir_cols = jnp.einsum(
        "crk,cks->crs", full_left, right_root, preferred_element_type=jnp.float32
    ).astype(jnp.bfloat16)
    outgoing = dir_cols.reshape(capacity, quarter, dp_count, sliver, half_width)
    outgoing = outgoing.transpose(0, 2, 1, 3, 4).reshape(capacity, block_width, half_width)
    returned = lax.all_to_all(outgoing, "dp", split_axis=1, concat_axis=0, tiled=True)
    other_cols = partner(returned, "mp", 0)
    left_cols = jnp.where(core_index == 0, returned, other_cols)
    right_cols = jnp.where(core_index == 0, other_cols, returned)
    slot_cols = jnp.concatenate([left_cols, right_cols], axis=2)
    slot_ids = jnp.arange(slot_block.shape[0], dtype=jnp.int32)
    block_range = jnp.arange(group_rows * block_cols, dtype=jnp.int32)
    matches = slot_block[None, :] == block_range[:, None]
    position = jnp.sum(jnp.where(matches, slot_ids[None, :], 0), axis=1)
    row_ids = jnp.arange(group_rows, dtype=jnp.int32)
    col_ids = jnp.arange(per_core, dtype=jnp.int32)
    my_blocks = (row_ids[:, None] * block_cols + core_index * per_core + col_ids[None, :]).reshape(
        -1
    )
    chosen = slot_cols[position[my_blocks]]
    restriped = chosen.reshape(group_rows, per_core, quarter, sliver, block_width)
    restriped = restriped.transpose(0, 2, 3, 1, 4).reshape(local_rows, local_cols)
    direction = lax.all_to_all(restriped, "dp", split_axis=0, concat_axis=0, tiled=True)
    return (direction, new_left, new_right)


def solution(mesh):
    return jax.shard_map(
        on_device,
        mesh=mesh,
        in_specs=(
            P("dp", "mp"),
            P(),
            P("dp", "mp", None),
            P("dp", "mp", None),
            P("dp", "mp", None),
            P("dp", None, "mp"),
        ),
        out_specs=(P("dp", "mp"), P("dp", "mp", None), P("dp", "mp", None)),
        check_vma=False,
    )
```

profile of v0, /device:TPU:1, one launch (start us, length us, event | category | flops | bytes accessed | tf_op | source)
XLA Modules:
  0.0 310.4 jit_solution(6362141050938546091)
XLA Ops:
  0.7 4.0 %all_to_all.30 = bf16[64,4,3072]{2,1,0:T(4,128)(2,1)} reshape(bf16[256,3072]{1,0:T(8,128)(2,1)} %param.6) | data formatting | bytes 3145728 | tf_op jit(solution)/shard_map/all_to_all | solution.py:29
  4.7 12.2 %all-to-all-start = ((bf16[64,4,3072]{2,1,0:T(4,128)(2,1)}), bf16[64,4,3072]{2,1,0:T(4,128)(2,1)}, u32[]{:S(2)}, u32[]{:S(2)}) async-start(bf16[64,4,3072]{2,1,0:T(4,128)(2,1)} %all_to_all.30), calls=%async_computation | async-start | bytes 3145728 | tf_op jit(solution)/shard_map/all_to_all | solution.py:29
  18.0 21.8 %all-to-all-done = bf16[64,4,3072]{2,1,0:T(4,128)(2,1)} async-done(((bf16[64,4,3072]{2,1,0:T(4,128)(2,1)}), bf16[64,4,3072]{2,1,0:T(4,128)(2,1)}, u32[]{:S(2)}, u32[]{:S(2)}) %all-to-all-start) | async-done | bytes 1572896 | tf_op jit(solution)/shard_map/all_to_all | solution.py:29
  42.8 5.6 %reshape.106 = bf16[16,4,4,3,1024]{4,3,1,0,2:T(4,128)(2,1)} reshape(bf16[64,4,3072]{2,0,1:T(8,128)(2,1)} %copy.60) | data formatting | bytes 3145728 | tf_op jit(solution)/shard_map/reshape | solution.py:30
  48.4 4.9 %copy.61 = bf16[16,3,4,4,1024]{4,3,2,1,0:T(4,128)(2,1)} copy(bf16[16,3,4,4,1024]{4,1,2,0,3:T(4,128)(2,1)} %bitcast.65) | data formatting | bytes 3145728 | tf_op jit(solution)/shard_map/transpose | solution.py:31
  53.2 3.5 %reshape.107 = bf16[48,16,1024]{2,1,0:T(8,128)(2,1)} reshape(bf16[16,3,4,4,1024]{4,3,2,1,0:T(4,128)(2,1)} %copy.61) | data formatting | bytes 3145728 | tf_op jit(solution)/shard_map/reshape | solution.py:31
  56.7 4.2 %gather_fusion = bf16[128,16,1024]{2,1,0:T(8,128)(2,1)} fusion(bf16[48,16,1024]{2,1,0:T(8,128)(2,1)} %reshape.107, s32[1024]{0:T(1024)S(1)} %pad_clamp_fusion.2), kind=kCustom, calls=%fused_computation | custom fusion | bytes 8389120 | tf_op jit(solution)/shard_map/gather | solution.py:39
  60.9 4.6 %broadcast_select_fusion = bf16[2,64,16,1024]{3,2,1,0:T(8,128)(2,1)} fusion(bf16[2,64,16,1024]{3,2,1,0:T(8,128)(2,1)} %bitcast.64, pred[2,64]{1,0:T(4,128)(4,1)S(1)} %bitcast_and_fusion.1), kind=kLoop, calls=%fused_computation.12 | loop fusion | flops 2097152 | bytes 8388736 | tf_op jit(solution)/shard_map/jit(_where)/select_n | solution.py:40
  65.5 6.5 %copy.64 = bf16[2,64,16,1024]{3,0,2,1:T(2,128)(2,1)S(1)} copy(bf16[2,64,16,1024]{3,2,1,0:T(8,128)(2,1)} %broadcast_select_fusion) | data formatting | bytes 8388608 | tf_op jit(solution)/shard_map/jit(_where)/select_n | solution.py:40
  72.0 4.7 %broadcast_in_dim.43 = bf16[2,64,2,16,1024]{4,0,3,2,1:T(2,128)(2,1)S(1)} broadcast(bf16[2,64,16,1024]{3,0,2,1:T(2,128)(2,1)S(1)} %copy.64), dimensions={0,1,3,4} | broadcast | bytes 12582912 | tf_op jit(solution)/shard_map/broadcast_in_dim | solution.py:41
  76.7 103.4 %all_to_all.44 = bf16[2,2048,1024]{2,0,1:T(2,128)(2,1)S(1)} all-to-all(bf16[2,2048,1024]{2,0,1:T(2,128)(2,1)S(1)} %bitcast.62), channel_id=1, replica_groups=mesh['dp'=64,'mp'=2] {'dp','mp'}, dimensions={1} | all-to-all | bytes 16777216 | tf_op jit(solution)/shard_map/all_to_all | solution.py:43
  180.1 4.4 %fusion = bf16[2,4,64,4,1024]{4,0,3,1,2:T(2,128)(2,1)S(1)} fusion(bf16[2,64,2,4,4,1024]{5,0,4,3,2,1:T(2,128)(2,1)S(1)} %bitcast.63), kind=kLoop, calls=%fused_computation.4 | loop fusion | flops 2097152 | bytes 12582912 | tf_op jit(solution)/shard_map/transpose | solution.py:46
  184.6 3.6 %copy.65 = bf16[2,4,64,4,1024]{4,3,2,1,0:T(4,128)(2,1)} copy(bf16[2,4,64,4,1024]{4,0,3,1,2:T(2,128)(2,1)S(1)} %fusion) | data formatting | bytes 8388608 | tf_op jit(solution)/shard_map/transpose | solution.py:46
  188.2 6.9 %reshape.110 = bf16[2,1024,1024]{2,1,0:T(8,128)(2,1)} reshape(bf16[2,4,64,4,1024]{4,3,2,1,0:T(4,128)(2,1)} %copy.65) | data formatting | bytes 8388608 | tf_op jit(solution)/shard_map/reshape | solution.py:46
  195.1 5.8 %convert_bitcast_fusion = bf16[2,512,1024]{2,1,0:T(8,128)(2,1)} fusion(bf16[2,512,1024]{2,1,0:T(8,128)(2,1)S(1)} %copy-done, bf16[2,1024,1024]{2,1,0:T(8,128)(2,1)} %reshape.110), kind=kOutput, calls=%fused_computation.15 | convolution fusion | flops 2148532224 | bytes 8388608 | tf_op jit(solution)/shard_map/crk,cks->crs/dot_general | solution.py:55
  201.9 4.0 %collective-permute-done = bf16[2,512,1024]{2,1,0:T(8,128)(2,1)S(1)} collective-permute-done((bf16[2,512,1024]{2,1,0:T(8,128)(2,1)}, bf16[2,512,1024]{2,1,0:T(8,128)(2,1)S(1)}, u32[]{:S(2)}, u32[]{:S(2)}) %collective-permute-start) | collective-permute-done | bytes 2097184 | tf_op jit(solution)/shard_map/ppermute | solution.py:12
  207.7 3.6 %fusion.7 = bf16[2,1024,512]{2,1,0:T(8,128)(2,1)} fusion(bf16[2,1024,512]{2,1,0:T(8,128)(2,1)S(1)} %copy-done.4, bf16[2,512,1024]{2,1,0:T(8,128)(2,1)S(1)} %get-tuple-element.6, bf16[2,512,1024]{2,1,0:T(8,128)(2,1)S(1)} %get-tuple-element.5), kind=kOutput, calls=%fused_computation.20 | convolution fusion | flops 2156920832 | bytes 8388608 | tf_op jit(solution)/shard_map/crk,cks->crs/dot_general | solution.py:62
  213.9 3.2 %copy.66 = bf16[2,4,64,4,512]{4,0,3,1,2:T(2,128)(2,1)S(1)} copy(bf16[2,4,64,4,512]{4,3,2,1,0:T(4,128)(2,1)S(1)} %reshape.111) | data formatting | bytes 4194304 | tf_op jit(solution)/shard_map/reshape | solution.py:65
  217.2 35.6 %all_to_all.45 = bf16[2,1024,512]{2,0,1:T(2,128)(2,1)S(1)} all-to-all(bf16[2,1024,512]{2,0,1:T(2,128)(2,1)S(1)} %bitcast.66), channel_id=1, replica_groups=mesh['dp'=64,'mp'=2] {'dp'}, dimensions={1} | all-to-all | bytes 4194304 | tf_op jit(solution)/shard_map/all_to_all | solution.py:67
  277.4 5.5 %all-to-all-start.3 = ((bf16[64,4,3072]{2,1,0:T(4,128)(2,1)}), bf16[64,4,3072]{2,1,0:T(4,128)(2,1)}, u32[]{:S(2)}, u32[]{:S(2)}) async-start(bf16[64,4,3072]{2,1,0:T(4,128)(2,1)} %reshape.140), calls=%async_computation.3 | async-start | bytes 3145728 | tf_op jit(solution)/shard_map/all_to_all | solution.py:84
  282.9 8.8 %multiply_add_fusion = f32[2,512,1024]{2,1,0:T(8,128)} fusion(f32[2,512,1024]{2,1,0:T(8,128)} %param.9, bf16[2,1024,1024]{2,1,0:T(8,128)(2,1)} %reshape.110, s32[]{:T(128)S(6)} %select_n.97), kind=kOutput, calls=%fused_computation.10 | convolution fusion | flops 2150629376 | bytes 14680068 | tf_op jit(solution)/shard_map/ckr,cks->crs/dot_general | solution.py:50
  291.7 4.6 %multiply_add_fusion.1 = f32[2,512,1024]{2,1,0:T(8,128)} fusion(f32[2,512,1024]{2,1,0:T(8,128)S(1)} %copy-done.3, bf16[2,1024,1024]{2,1,0:T(8,128)(2,1)S(1)} %copy-done.2, s32[]{:T(128)S(6)} %select_n.97), kind=kOutput, calls=%fused_computation.11 | convolution fusion | flops 2150629376 | bytes 14680068 | tf_op jit(solution)/shard_map/crk,csk->crs/dot_general | solution.py:49
  296.3 10.4 %all-to-all-done.3 = bf16[64,4,3072]{2,1,0:T(4,128)(2,1)} async-done(((bf16[64,4,3072]{2,1,0:T(4,128)(2,1)}), bf16[64,4,3072]{2,1,0:T(4,128)(2,1)}, u32[]{:S(2)}, u32[]{:S(2)}) %all-to-all-start.3) | async-done | bytes 1572896 | tf_op jit(solution)/shard_map/all_to_all | solution.py:84
  306.7 3.7 %all_to_all.39 = bf16[256,3072]{1,0:T(8,128)(2,1)} reshape(bf16[64,4,3072]{2,1,0:T(4,128)(2,1)} %all-to-all-done.3) | data formatting | bytes 3145728 | tf_op jit(solution)/shard_map/all_to_all | solution.py:84
  (49 shorter events, 34.0 us)
Async XLA Ops:
  0.6 194.4 %copy-start = (bf16[2,512,1024]{2,1,0:T(8,128)(2,1)S(1)}, bf16[2,512,1024]{2,1,0:T(8,128)(2,1)}, u32[]{:S(2)}) copy-start(bf16[2,512,1024]{2,1,0:T(8,128)(2,1)} %param.10) | copy-start | bytes 6291460
  0.6 16.2 %copy-start.5 = (s32[128]{0:T(128)S(1)}, s32[128]{0:T(128)}, u32[]{:S(2)}) copy-start(s32[128]{0:T(128)} %param.7) | copy-start | bytes 1540
  4.7 35.1 %all-to-all-start = ((bf16[64,4,3072]{2,1,0:T(4,128)(2,1)}), bf16[64,4,3072]{2,1,0:T(4,128)(2,1)}, u32[]{:S(2)}, u32[]{:S(2)}) async-start(bf16[64,4,3072]{2,1,0:T(4,128)(2,1)} %all_to_all.30), calls=%async_computation | async-start | bytes 3145728 | tf_op jit(solution)/shard_map/all_to_all | solution.py:29
  200.9 4.9 %collective-permute-start = (bf16[2,512,1024]{2,1,0:T(8,128)(2,1)}, bf16[2,512,1024]{2,1,0:T(8,128)(2,1)S(1)}, u32[]{:S(2)}, u32[]{:S(2)}) collective-permute-start(bf16[2,512,1024]{2,1,0:T(8,128)(2,1)} %convert_bitcast_fusion), channel_id=1, source_target_pairs={{0,1},{1,0},{2,3},{3,2},{4,5},{5,4},{6,7},{7,6},{8,9},{9,8},{10,11... | collective-permute-start | bytes 6291464 | tf_op jit(solution)/shard_map/ppermute | solution.py:12
  201.9 5.9 %copy-start.4 = (bf16[2,1024,512]{2,1,0:T(8,128)(2,1)S(1)}, bf16[2,1024,512]{2,1,0:T(8,128)(2,1)}, u32[]{:S(2)}) copy-start(bf16[2,1024,512]{2,1,0:T(8,128)(2,1)} %param.11) | copy-start | bytes 6291460
  254.7 6.7 %collective-permute-start.1 = (bf16[128,16,512]{2,1,0:T(8,128)(2,1)}, bf16[128,16,512]{2,1,0:T(8,128)(2,1)}, u32[]{:S(2)}, u32[]{:S(2)}) collective-permute-start(bf16[128,16,512]{2,1,0:T(8,128)(2,1)} %bitcast.15), channel_id=1, source_target_pairs={{0,1},{1,0},{2,3},{3,2},{4,5},{5,4},{6,7},{7,6},{8,9},{9,8},{10,11... | collective-permute-start | bytes 6291464 | tf_op jit(solution)/shard_map/ppermute | solution.py:12
  277.4 29.4 %all-to-all-start.3 = ((bf16[64,4,3072]{2,1,0:T(4,128)(2,1)}), bf16[64,4,3072]{2,1,0:T(4,128)(2,1)}, u32[]{:S(2)}, u32[]{:S(2)}) async-start(bf16[64,4,3072]{2,1,0:T(4,128)(2,1)} %reshape.140), calls=%async_computation.3 | async-start | bytes 3145728 | tf_op jit(solution)/shard_map/all_to_all | solution.py:84
  282.9 8.8 %copy-start.2 = (bf16[2,1024,1024]{2,1,0:T(8,128)(2,1)S(1)}, bf16[2,1024,1024]{2,1,0:T(8,128)(2,1)}, u32[]{:S(2)}) copy-start(bf16[2,1024,1024]{2,1,0:T(8,128)(2,1)} %reshape.110) | copy-start | bytes 12582916
  282.9 8.8 %copy-start.3 = (f32[2,512,1024]{2,1,0:T(8,128)S(1)}, f32[2,512,1024]{2,1,0:T(8,128)}, u32[]{:S(2)}) copy-start(f32[2,512,1024]{2,1,0:T(8,128)} %param.8) | copy-start | bytes 12582916
  291.7 18.8 %copy-start.1 = (bf16[2,512,1024]{2,1,0:T(8,128)(2,1)S(1)}, bf16[2,512,1024]{2,1,0:T(8,128)(2,1)}, u32[]{:S(2)}) copy-start(bf16[2,512,1024]{2,1,0:T(8,128)(2,1)} %param.10) | copy-start | bytes 6291460
where the time goes:
time: 312 us; the launch traced here: 310 us
  blocking collectives  139 us (45%)
  local copies, waits for them, and re-layouts  71 us (23%)
  waiting for transfers between devices  39.2 us (13%)
  matrix products  22.9 us (7%)
  starting transfers between devices  21.2 us (7%)
  other arithmetic  16.2 us (5%)
    all_to_all x1, blocking collectives, on_device(): lax.all_to_all(doubled, ('dp', 'mp'), split_axis=1, concat_axis=1, tiled=...  103 us
    all_to_all x1, blocking collectives, on_device(): lax.all_to_all(outgoing, 'dp', split_axis=1, concat_axis=0, tiled=True)  35.6 us
    all_to_all x1, waiting for transfers between devices, on_device(): lax.all_to_all(grads, 'dp', split_axis=0, concat_axis=0, tiled=True)  21.8 us
    all_to_all x1, starting transfers between devices, on_device(): lax.all_to_all(grads, 'dp', split_axis=0, concat_axis=0, tiled=True)  12.2 us
    all_to_all x1, waiting for transfers between devices, on_device(): lax.all_to_all(restriped, 'dp', split_axis=0, concat_axis=0, tiled=True)  10.4 us
    all_to_all x3, local copies, waits for them, and re-layouts, on_device(): lax.all_to_all(restriped, 'dp', split_axis=0, concat_axis=0, tiled=True)  9.72 us
    dot_general x1, matrix products, on_device(): jnp.einsum('ckr,cks->crs', own_cols, full_block, preferred_element_type=j...  8.77 us
    all_to_all x2, local copies, waits for them, and re-layouts, on_device(): lax.all_to_all(grads, 'dp', split_axis=0, concat_axis=0, tiled=True)  7.03 us
  transfers between devices with their start and end apart: 4, of which 4 were waited for; matrix products, arithmetic and copies ran while one was open for 5% of the time, Pallas kernels for 0%

commit v1 on v0

v1 whole, which is shorter than its diff:
```python
import functools

import jax
import jax.numpy as jnp
from jax import lax
from jax.experimental import pallas as pl
from jax.experimental.pallas import tpu as pltpu
from jax.sharding import PartitionSpec as P

MESH = pl.DeviceIdType.MESH
KEEP = 0.9
SIDE = 4
CHIPS = SIDE**3
PLANE = SIDE**2
BS = 1024
HALF = 512
QUARTER = 256
BLOCKS = 96
SLOTS = 128
SLIVER = 16
CHUNKS = 2
W = HALF // CHUNKS


def negated(offset):
    return tuple(-v % SIDE for v in offset)


def rotated(offset, by):
    return tuple(offset[(i - by) % 3] for i in range(3))


def cube_order():
    order = []
    for a in (1, 3):
        for b in (1, 3):
            order += [(1, a, b), negated((1, a, b))]
    order.append((2, 2, 2))
    for by in range(3):
        for a in (1, 3):
            for offset in (rotated((1, a, 2), by), rotated((1, a, 0), by)):
                order += [offset, negated(offset)]
        for offset in (rotated((1, 2, 2), by), rotated((1, 0, 0), by)):
            order += [offset, negated(offset)]
        order += [rotated((2, 2, 0), by), rotated((0, 0, 2), by)]
    for start in ((1, 2, 0), (1, 0, 2)):
        for by in range(3):
            offset = rotated(start, by)
            order += [offset, negated(offset)]
    return order


def plane_order():
    order = []
    for offset in ((1, 1, 0), (1, 3, 0), (1, 2, 0), (2, 1, 0), (1, 0, 0), (0, 1, 0)):
        order += [offset, negated(offset)]
    return order[:4] + [(2, 2, 0)] + order[4:] + [(2, 0, 0), (0, 2, 0)]


def kernel(
    ids, pos, grads, left_stats, right_stats, left_root, right_root,
    direction, new_left, new_right,
    window, spread, routed, block, left, right, part, result, back, chosen, final, sum_left, sum_right,
    load_sem, store_sem, local_sem, send_sem, recv_sem, line_sem,
):
    dp, me = lax.axis_index("dp"), lax.axis_index("mp")
    y, z, x = dp // PLANE, (dp // SIDE) % SIDE, dp % SIDE
    other = 1 - me
    strip = y * SIDE + z
    my_rows = pl.ds(pl.multiple_of(x * QUARTER + strip * SLIVER, SLIVER), SLIVER)

    def chip(offset):
        a, b, c = (y + offset[0]) % SIDE, (z + offset[1]) % SIDE, (x + offset[2]) % SIDE
        return (a * SIDE + b) * SIDE + c, a * SIDE + b, c

    def cols(core, c):
        return pl.ds(pl.multiple_of(core * HALF + c * W, 128), W)

    def remote(src, dst, sem, device):
        return pltpu.make_async_remote_copy(
            src_ref=src, dst_ref=dst, send_sem=send_sem.at[sem], recv_sem=recv_sem.at[sem],
            device_id=device, device_id_type=MESH,
        )

    P1, P2, P3, P4, LP, GX, LX = (CHUNKS * i for i in range(7))

    loads = [
        pltpu.make_async_copy(grads.at[:, pl.ds(j * BS, BS)], window.at[j], load_sem.at[j]) for j in range(3)
    ]
    my_half = pl.ds(pl.multiple_of(me * HALF, HALF), HALF)
    load_left = pltpu.make_async_copy(left_root, left.at[:, my_half, :], load_sem.at[3])
    load_right = pltpu.make_async_copy(right_root, right, load_sem.at[4])
    load_sl = pltpu.make_async_copy(left_stats, sum_left, load_sem.at[5])
    load_sr = pltpu.make_async_copy(right_stats, sum_right, load_sem.at[6])
    for load in loads:
        load.start()

    barrier = pltpu.get_barrier_semaphore()
    greeted = 0
    for offset in plane_order():
        for core in (me, other):
            pl.semaphore_signal(barrier, inc=1, device_id=(chip(offset)[0], core), device_id_type=MESH)
            greeted += 1
    line = [(chip((0, 0, c))[0], me) for c in (1, 2, 3)]
    for device in [(dp, other)] + line:
        pl.semaphore_signal(barrier, inc=1, device_id=device, device_id_type=MESH)
        greeted += 1
    load_left.start()
    load_right.start()
    load_sl.start()
    load_sr.start()
    for c in range(CHUNKS):
        spread[c][BLOCKS] = jnp.zeros((SLIVER, W), jnp.bfloat16)
    pl.semaphore_wait(barrier, greeted)
    for device in line:
        pl.semaphore_signal(line_sem, inc=1, device_id=device, device_id_type=MESH)

    for load in loads:
        load.wait()
    mine = pl.ds(strip * 6 + me * 3, 3)
    locals_ = []
    for c in range(CHUNKS):
        for offset in plane_order() + [(0, 0, 0)]:
            to, to_strip, _ = chip(offset)
            rows = pl.ds(pl.multiple_of(to_strip * SLIVER, SLIVER), SLIVER)
            for core in (me, other):
                src, dst = window.at[:, rows, cols(core, c)], spread[c].at[mine]
                if any(offset) or core is other:
                    remote(src, dst, P1 + c, (to, core)).start()
                else:
                    copy = pltpu.make_async_copy(src, dst, local_sem.at[P1 + c])
                    copy.start()
                    locals_.append(copy)

    load_left.wait()
    send_left = remote(left.at[:, my_half, :], left.at[:, my_half, :], LX, (dp, other))
    send_left.start()

    pl.semaphore_wait(line_sem, 3)
    routes = []
    for c in range(CHUNKS):
        remote(spread[c].at[pl.ds(0, 93)], spread[c].at[pl.ds(0, 93)], P1 + c, (dp, other)).wait_recv()
        locals_[c].wait()

        def pick(slot, _):
            routed[c, slot] = spread[c][ids[slot]]
            return 0

        lax.fori_loop(0, SLOTS, pick, 0, unroll=8)
        for offset in cube_order():
            to, _, _ = chip(offset)
            remote(
                routed.at[c, pl.ds(2 * to, 2)], block.at[:, my_rows, cols(me, c)], P2 + c, (to, me)
            ).start()
        copy = pltpu.make_async_copy(
            routed.at[c, pl.ds(2 * dp, 2)], block.at[:, my_rows, cols(me, c)], local_sem.at[P2 + c]
        )
        copy.start()
        routes.append(copy)

    load_right.wait()
    exchanges = []
    for c in range(CHUNKS):
        remote(routed.at[c, pl.ds(0, 126)], routed.at[c, pl.ds(0, 126)], P2 + c, (dp, other)).wait_recv()
        routes[c].wait()
        here = cols(me, c)
        send_block = remote(block.at[:, :, here], block.at[:, :, here], GX + c, (dp, other))
        send_block.start()
        if c == 0:
            send_left.wait_recv()

        def left_tile(i, _):
            s, r = i // 4, i % 4
            rows = pl.ds(pl.multiple_of(r * 256, 256), 256)
            part[s, rows, here] = jnp.dot(
                left[s, rows, :], block[s, :, here], preferred_element_type=jnp.float32
            ).astype(jnp.bfloat16)
            return 0

        lax.fori_loop(0, 8, left_tile, 0)
        send_part = remote(part.at[:, :, here], part.at[:, :, here], LP + c, (dp, other))
        send_part.start()
        exchanges += [send_part, send_block]
    for c in range(CHUNKS):
        exchanges[2 * c].wait_recv()

    homes = []
    for c in range(CHUNKS):
        def dir_tile(i, _):
            s, r = i // 4, i % 4
            rows = pl.ds(pl.multiple_of(r * 256, 256), 256)
            result[s, rows, pl.ds(c * W, W)] = jnp.dot(
                part[s, rows, :], right[s, :, pl.ds(c * W, W)], preferred_element_type=jnp.float32
            ).astype(jnp.bfloat16)
            return 0

        lax.fori_loop(0, 8, dir_tile, 0)
        for offset in cube_order():
            to, to_strip, to_x = chip(offset)
            rows = pl.ds(pl.multiple_of(to_x * QUARTER + to_strip * SLIVER, SLIVER), SLIVER)
            remote(
                result.at[:, rows, pl.ds(c * W, W)], back[c].at[pl.ds(2 * dp, 2)], P3 + c, (to, me)
            ).start()
        copy = pltpu.make_async_copy(
            result.at[:, my_rows, pl.ds(c * W, W)], back[c].at[pl.ds(2 * dp, 2)], local_sem.at[P3 + c]
        )
        copy.start()
        homes.append(copy)

    for c in range(CHUNKS):
        exchanges[2 * c + 1].wait_recv()
    load_sl.wait()
    load_sr.wait()

    def gram_left(i, _):
        s, r, n = i // 4, (i // 2) % 2, i % 2
        rows = pl.ds(pl.multiple_of(r * 256, 256), 256)
        own = pl.ds(pl.multiple_of(me * HALF + r * 256, 256), 256)
        to = pl.ds(pl.multiple_of(n * 512, 512), 512)
        gram = lax.dot_general(
            block[s, own, :], block[s, to, :], (((1,), (1,)), ((), ())), preferred_element_type=jnp.float32
        )
        sum_left[s, rows, to] = KEEP * sum_left[s, rows, to] + (1.0 - KEEP) * gram
        return 0

    def gram_right(i, _):
        s, r, n = i // 4, (i // 2) % 2, i % 2
        rows = pl.ds(pl.multiple_of(r * 256, 256), 256)
        own = pl.ds(pl.multiple_of(me * HALF + r * 256, 256), 256)
        to = pl.ds(pl.multiple_of(n * 512, 512), 512)
        gram = lax.dot_general(
            block[s, :, own], block[s, :, to], (((0,), (0,)), ((), ())), preferred_element_type=jnp.float32
        )
        sum_right[s, rows, to] = KEEP * sum_right[s, rows, to] + (1.0 - KEEP) * gram
        return 0

    lax.fori_loop(0, 8, gram_left, 0)
    store_left = pltpu.make_async_copy(sum_left, new_left, store_sem.at[0])
    store_left.start()
    lax.fori_loop(0, 8, gram_right, 0)
    store_right = pltpu.make_async_copy(sum_right, new_right, store_sem.at[1])
    store_right.start()

    ends = []
    for c in range(CHUNKS):
        remote(back[c].at[pl.ds(0, 126)], back[c].at[pl.ds(0, 126)], P3 + c, (dp, other)).wait_recv()
        homes[c].wait()

        def choose(b, _):
            chosen[c, b] = back[c][pos[b]]
            return 0

        lax.fori_loop(0, BLOCKS, choose, 0, unroll=8)
        rows = pl.ds(pl.multiple_of(strip * SLIVER, SLIVER), SLIVER)
        for offset in plane_order() + [(0, 0, 0)]:
            to, to_strip, _ = chip(offset)
            for core in (me, other):
                src, dst = chosen.at[c, pl.ds(to_strip * 6 + core * 3, 3)], final.at[:, rows, cols(me, c)]
                if any(offset) or core is other:
                    remote(src, dst, P4 + c, (to, core)).start()
                else:
                    copy = pltpu.make_async_copy(src, dst, local_sem.at[P4 + c])
                    copy.start()
                    ends.append(copy)
    stores = []
    for c in range(CHUNKS):
        remote(chosen.at[c, pl.ds(0, 93)], chosen.at[c, pl.ds(0, 93)], P4 + c, (dp, other)).wait_recv()
        ends[c].wait()
        for j in range(3):
            for core in range(2):
                at = core * HALF + c * W
                copy = pltpu.make_async_copy(
                    final.at[j, :, pl.ds(at, W)], direction.at[:, pl.ds(j * BS + at, W)],
                    store_sem.at[2 + (c * 3 + j) * 2 + core],
                )
                copy.start()
                stores.append(copy)

    for c in range(CHUNKS):
        remote(spread[c].at[pl.ds(0, 93)], spread[c].at[pl.ds(0, 93)], P1 + c, (dp, other)).wait_send()
        remote(routed.at[c, pl.ds(0, 126)], routed.at[c, pl.ds(0, 126)], P2 + c, (dp, other)).wait_send()
        remote(back[c].at[pl.ds(0, 126)], back[c].at[pl.ds(0, 126)], P3 + c, (dp, other)).wait_send()
        remote(chosen.at[c, pl.ds(0, 93)], chosen.at[c, pl.ds(0, 93)], P4 + c, (dp, other)).wait_send()
    send_left.wait_send()
    for copy in exchanges:
        copy.wait_send()
    for copy in [store_left, store_right] + stores:
        copy.wait()


def on_device(grads, slot_block, left_stats, right_stats, left_root, right_root):
    ids = jnp.where(slot_block >= 0, slot_block, BLOCKS).astype(jnp.int32)
    matches = slot_block[None, :] == jnp.arange(BLOCKS, dtype=jnp.int32)[:, None]
    pos = jnp.sum(jnp.where(matches, jnp.arange(SLOTS, dtype=jnp.int32)[None, :], 0), axis=1)
    bf16 = jnp.bfloat16
    anywhere = pl.BlockSpec(memory_space=pl.ANY)
    scalars = pl.BlockSpec(memory_space=pltpu.SMEM)
    outs = [(grads.shape, bf16), (left_stats.shape, jnp.float32), (right_stats.shape, jnp.float32)]
    return pl.pallas_call(
        kernel,
        out_shape=[jax.ShapeDtypeStruct(*out) for out in outs],
        in_specs=[scalars] * 2 + [anywhere] * 5,
        out_specs=[anywhere] * 3,
        scratch_shapes=[
            pltpu.VMEM((3, QUARTER, BS), bf16),
            [pltpu.VMEM((BLOCKS + 1, SLIVER, W), bf16) for _ in range(CHUNKS)],
            pltpu.VMEM((CHUNKS, SLOTS, SLIVER, W), bf16),
            pltpu.VMEM((2, BS, BS), bf16),
            pltpu.VMEM((2, BS, BS), bf16),
            pltpu.VMEM((2, BS, HALF), bf16),
            pltpu.VMEM((2, BS, BS), bf16),
            pltpu.VMEM((2, BS, HALF), bf16),
            [pltpu.VMEM((SLOTS, SLIVER, W), bf16) for _ in range(CHUNKS)],
            pltpu.VMEM((CHUNKS, BLOCKS, SLIVER, W), bf16),
            pltpu.VMEM((3, QUARTER, BS), bf16),
            pltpu.VMEM((2, HALF, BS), jnp.float32),
            pltpu.VMEM((2, HALF, BS), jnp.float32),
            pltpu.SemaphoreType.DMA((7,)),
            pltpu.SemaphoreType.DMA((2 + 6 * CHUNKS,)),
            pltpu.SemaphoreType.DMA((4 * CHUNKS,)),
            pltpu.SemaphoreType.DMA((7 * CHUNKS,)),
            pltpu.SemaphoreType.DMA((7 * CHUNKS,)),
            pltpu.SemaphoreType.REGULAR,
        ],
        compiler_params=pltpu.CompilerParams(
            collective_id=0, has_side_effects=True, vmem_limit_bytes=60 * 2**20
        ),
    )(ids, pos, grads, left_stats, right_stats, left_root, right_root)


def solution(mesh):
    return jax.shard_map(
        on_device,
        mesh=mesh,
        in_specs=(
            P("dp", "mp"),
            P(),
            P("dp", "mp", None),
            P("dp", "mp", None),
            P("dp", "mp", None),
            P("dp", None, "mp"),
        ),
        out_specs=(P("dp", "mp"), P("dp", "mp", None), P("dp", "mp", None)),
        check_vma=False,
    )
```

time: 312 us -> 118 us (0.38)
  blocking collectives: 139 us -> 0 us
  Pallas kernels: 0 us -> 105 us
  local copies, waits for them, and re-layouts: 71 us -> 9.61 us
  waiting for transfers between devices: 39.2 us -> 0 us
  matrix products: 22.9 us -> 0 us
  starting transfers between devices: 21.2 us -> 0 us
  other arithmetic: 16.2 us -> 2.45 us
    all_to_all x2 -> x0, blocking collectives: 139 us -> none  [the longest x1 103 us: on_device(): lax.all_to_all(doubled, ('dp', 'mp'), split_axis=1, concat_axis=1, tiled=...]
    pallas_call x0 -> x1, Pallas kernels: none -> 105 us  [on_device(): pl.pallas_call(kernel, out_shape=[jax.ShapeDtypeStruct(*out) for out in o...]
    all_to_all x2 -> x0, waiting for transfers between devices: 32.2 us -> none  [the longest x1 21.8 us: on_device(): lax.all_to_all(grads, 'dp', split_axis=0, concat_axis=0, tiled=True)]
    reshape x6 -> x0, local copies, waits for them, and re-layouts: 23.7 us -> none  [the longest x1 6.87 us: on_device(): merged.transpose(0, 2, 1, 3, 4).reshape(capacity, block_width, block_width)]
    dot_general x4 -> x0, matrix products: 22.9 us -> none  [the longest x1 8.77 us: on_device(): jnp.einsum('ckr,cks->crs', own_cols, full_block, preferred_element_type=j...]
    all_to_all x7 -> x0, local copies, waits for them, and re-layouts: 18.6 us -> none  [the longest x3 9.72 us: on_device(): lax.all_to_all(restriped, 'dp', split_axis=0, concat_axis=0, tiled=True)]
    all_to_all x2 -> x0, starting transfers between devices: 17.7 us -> none  [the longest x1 12.2 us: on_device(): lax.all_to_all(grads, 'dp', split_axis=0, concat_axis=0, tiled=True)]
    unnamed x12 -> x5, local copies, waits for them, and re-layouts: 0.04 us -> 9.61 us
  transfers between devices with their start and end apart: 4 -> 0, of which waited for: 4 -> 0; matrix products, arithmetic and copies ran while one was open for 5% -> 0% of each run, Pallas kernels for 0% -> 0%
where the time goes in v1:
time: 118 us
  Pallas kernels  105 us (89%)
  local copies, waits for them, and re-layouts  9.61 us (8%)
  other arithmetic  2.45 us (2%)
    pallas_call x1, Pallas kernels, on_device(): pl.pallas_call(kernel, out_shape=[jax.ShapeDtypeStruct(*out) for out in o...  105 us
    unnamed x5, local copies, waits for them, and re-layouts  9.61 us

profile of v1, /device:TPU:1, one launch (start us, length us, event | category | flops | bytes accessed | tf_op | source)
XLA Modules:
  0.0 118.0 jit_solution(16856048472590590944)
XLA Ops:
  0.6 1.3 %select_reduce_fusion.pos = s32[96]{0:T(128)} fusion(s32[128]{0:T(128)} %param.7), kind=kLoop, calls=%fused_computation | loop fusion | flops 36768 | bytes 896 | tf_op jit(solution)/shard_map/reduce_sum | solution.py:294
  1.9 1.2 compare_select_fusion.ids
  3.1 105.3 %shard_map.85 = (bf16[256,3072]{1,0:T(8,128)(2,1)}, f32[2,512,1024]{2,1,0:T(8,128)}, f32[2,512,1024]{2,1,0:T(8,128)}) custom-call(s32[128]{0:T(128)} %compare_select_fusion.ids, s32[96]{0:T(128)} %select_reduce_fusion.pos, bf16[256,3072]{1,0:T(8,128)(2,1)} %grads.1, f32[2,512,1024]{2,1,0:T(8,128)} %left_stats.1, f32[2,512,1024]{2,1,0:T(8,128)} %right_stats.1, ...), custom_call_target="tpu_custom_call" | custom-call | tf_op jit(solution)/shard_map/pallas_call | solution.py:299
  108.4 2.7 %copy.12 = bf16[256,3072]{1,0:T(8,128)(2,1)} copy(bf16[256,3072]{1,0:T(8,128)(2,1)} %get-tuple-element.6) | data formatting | bytes 3145728
  111.1 0.0 copy-start
  111.1 4.9 %copy.13 = f32[2,512,1024]{2,1,0:T(8,128)} copy(f32[2,512,1024]{2,1,0:T(8,128)} %get-tuple-element.7) | data formatting | bytes 8388608
  116.0 0.0 copy-done
  116.0 2.0 %copy.14 = f32[2,512,1024]{2,1,0:T(8,128)} copy(f32[2,512,1024]{2,1,0:T(8,128)S(1)} %copy-done) | data formatting | bytes 8388608
Async XLA Ops:
  111.1 4.9 %copy-start = (f32[2,512,1024]{2,1,0:T(8,128)S(1)}, f32[2,512,1024]{2,1,0:T(8,128)}, u32[]{:S(2)}) copy-start(f32[2,512,1024]{2,1,0:T(8,128)} %get-tuple-element.8) | copy-start | bytes 12582916

commit v2 on v1

v2 whole, which is shorter than its diff:
```python
import functools

import jax
import jax.numpy as jnp
from jax import lax
from jax.experimental import pallas as pl
from jax.experimental.pallas import tpu as pltpu
from jax.sharding import PartitionSpec as P

MESH = pl.DeviceIdType.MESH
KEEP = 0.9
SIDE = 4
CHIPS = SIDE**3
PLANE = SIDE**2
BS = 1024
HALF = 512
QUARTER = 256
BLOCKS = 96
SLOTS = 128
SLIVER = 16
CHUNKS = 2
W = HALF // CHUNKS


def negated(offset):
    return tuple(-v % SIDE for v in offset)


def rotated(offset, by):
    return tuple(offset[(i - by) % 3] for i in range(3))


def cube_order():
    order = []
    for a in (1, 3):
        for b in (1, 3):
            order += [(1, a, b), negated((1, a, b))]
    order.append((2, 2, 2))
    for by in range(3):
        for a in (1, 3):
            for offset in (rotated((1, a, 2), by), rotated((1, a, 0), by)):
                order += [offset, negated(offset)]
        for offset in (rotated((1, 2, 2), by), rotated((1, 0, 0), by)):
            order += [offset, negated(offset)]
        order += [rotated((2, 2, 0), by), rotated((0, 0, 2), by)]
    for start in ((1, 2, 0), (1, 0, 2)):
        for by in range(3):
            offset = rotated(start, by)
            order += [offset, negated(offset)]
    return order


def plane_order():
    order = []
    for offset in ((1, 1, 0), (1, 3, 0), (1, 2, 0), (2, 1, 0), (1, 0, 0), (0, 1, 0)):
        order += [offset, negated(offset)]
    return order[:4] + [(2, 2, 0)] + order[4:] + [(2, 0, 0), (0, 2, 0)]


def kernel(
    ids, grads, left_stats, right_stats, left_root, right_root,
    direction, new_left, new_right,
    window, spread, routed, block, left, right, part, result, back, chosen, table, places,
    load_sem, local_sem, send_sem, recv_sem, line_sem,
):
    dp, me = lax.axis_index("dp"), lax.axis_index("mp")
    y, z, x = dp // PLANE, (dp // SIDE) % SIDE, dp % SIDE
    other = 1 - me
    strip = y * SIDE + z
    my_rows = pl.ds(pl.multiple_of(x * QUARTER + strip * SLIVER, SLIVER), SLIVER)
    my_half = pl.ds(pl.multiple_of(me * HALF, HALF), HALF)
    drain = []

    def chip(offset):
        a, b, c = (y + offset[0]) % SIDE, (z + offset[1]) % SIDE, (x + offset[2]) % SIDE
        return (a * SIDE + b) * SIDE + c, a * SIDE + b, c

    def cols(core, c):
        return pl.ds(pl.multiple_of(core * HALF + c * W, 128), W)

    def remote(src, dst, sem, device):
        return pltpu.make_async_remote_copy(
            src_ref=src, dst_ref=dst, send_sem=send_sem.at[sem], recv_sem=recv_sem.at[sem],
            device_id=device, device_id_type=MESH,
        )

    def many(pieces, sem):
        span = routed.at[0, pl.ds(0, pieces)]
        return remote(span, span, sem, (dp, other))

    P1, P3, P4 = 0, CHUNKS, 2 * CHUNKS
    P2, PX, GX, LX = 3 * CHUNKS, 3 * CHUNKS + 2, 3 * CHUNKS + 4, 3 * CHUNKS + 6

    loads = [
        pltpu.make_async_copy(grads.at[:, pl.ds(j * BS, BS)], window.at[j], load_sem.at[j]) for j in range(3)
    ]
    load_left = pltpu.make_async_copy(left_root, left.at[:, my_half, :], load_sem.at[3])
    load_right = pltpu.make_async_copy(right_root, right, load_sem.at[4])
    load_sl = pltpu.make_async_copy(left_stats, new_left, load_sem.at[5])
    load_sr = pltpu.make_async_copy(right_stats, new_right, load_sem.at[6])
    for load in loads:
        load.start()

    barrier = pltpu.get_barrier_semaphore()
    greeted = 0
    for offset in plane_order():
        for core in (me, other):
            pl.semaphore_signal(barrier, inc=1, device_id=(chip(offset)[0], core), device_id_type=MESH)
            greeted += 1
    line = [(chip((0, 0, c))[0], me) for c in (1, 2, 3)]
    for device in [(dp, other)] + line:
        pl.semaphore_signal(barrier, inc=1, device_id=device, device_id_type=MESH)
        greeted += 1
    load_left.start()
    load_right.start()
    load_sl.start()
    load_sr.start()
    for c in range(CHUNKS):
        spread[c][BLOCKS] = jnp.zeros((SLIVER, W), jnp.bfloat16)
    pl.semaphore_wait(barrier, greeted)
    for device in line:
        pl.semaphore_signal(line_sem, inc=1, device_id=device, device_id_type=MESH)
    for load in loads:
        load.wait()
    mine = pl.ds(strip * 6 + me * 3, 3)
    kept = []
    for c in range(CHUNKS):
        for offset in plane_order() + [(0, 0, 0)]:
            to, to_strip, _ = chip(offset)
            rows = pl.ds(pl.multiple_of(to_strip * SLIVER, SLIVER), SLIVER)
            for core in (me, other):
                src, dst = window.at[:, rows, cols(core, c)], spread[c].at[mine]
                if any(offset) or core is other:
                    remote(src, dst, P1 + c, (to, core)).start()
                else:
                    kept.append(pltpu.make_async_copy(src, dst, local_sem.at[P1 + c]))
                    kept[-1].start()
        drain.append(many(93, P1 + c))

    load_left.wait()
    send_left = remote(left.at[:, my_half, :], left.at[:, my_half, :], LX, (dp, other))
    send_left.start()
    drain.append(send_left)

    lanes = lax.broadcasted_iota(jnp.int32, (8, SLOTS), 1)

    def seat(slot, seats):
        return jnp.where(lanes == ids[slot], slot, seats)

    table[...] = lax.fori_loop(0, SLOTS, seat, jnp.zeros((8, SLOTS), jnp.int32), unroll=8)
    fetch = pltpu.make_async_copy(table, places, load_sem.at[7])
    fetch.start()

    pl.semaphore_wait(line_sem, 3)

    def pick(c):
        many(93, P1 + c).wait_recv()
        kept[c].wait()

        def one(slot, _):
            held = ids[slot]
            routed[c, slot] = spread[c][jnp.where(held < 0, BLOCKS, held)]
            return 0

        lax.fori_loop(0, SLOTS, one, 0, unroll=8)

    arrivals = {}

    def route(c, s):
        for offset in cube_order():
            to, _, _ = chip(offset)
            remote(routed.at[c, 2 * to + s], block.at[s, my_rows, cols(me, c)], P2 + s, (to, me)).start()
        arrivals[c, s] = pltpu.make_async_copy(
            routed.at[c, 2 * dp + s], block.at[s, my_rows, cols(me, c)], local_sem.at[2 * CHUNKS + 2 * c + s]
        )
        arrivals[c, s].start()

    for c in range(CHUNKS):
        pick(c)
        route(c, 0)
    for c in range(CHUNKS):
        route(c, 1)
    fetch.wait()
    drain += [many(63 * CHUNKS, P2 + s) for s in range(2)]

    own = pl.ds(pl.multiple_of(me * HALF, HALF), HALF)
    exchanges = []

    def arrive(s):
        many(63 * CHUNKS, P2 + s).wait_recv()
        for c in range(CHUNKS):
            arrivals[c, s].wait()
        send_block = remote(block.at[s, :, own], block.at[s, :, own], GX + s, (dp, other))
        send_block.start()
        exchanges.append(send_block)
        drain.append(send_block)
        if s == 0:
            send_left.wait_recv()

        def left_tile(r, _):
            rows = pl.ds(pl.multiple_of(r * 256, 256), 256)
            part[s, rows, own] = jnp.dot(
                left[s, rows, :], block[s, :, own], preferred_element_type=jnp.float32
            ).astype(jnp.bfloat16)
            return 0

        lax.fori_loop(0, 4, left_tile, 0)
        send_part = remote(part.at[s, :, own], part.at[s, :, own], PX + s, (dp, other))
        send_part.start()
        drain.append(send_part)
        return send_part

    homes = {}

    def give_back(s, c):
        def dir_tile(r, _):
            rows = pl.ds(pl.multiple_of(r * 256, 256), 256)
            result[s, rows, pl.ds(c * W, W)] = jnp.dot(
                part[s, rows, :], right[s, :, pl.ds(c * W, W)], preferred_element_type=jnp.float32
            ).astype(jnp.bfloat16)
            return 0

        lax.fori_loop(0, 4, dir_tile, 0)
        for offset in cube_order():
            to, to_strip, to_x = chip(offset)
            rows = pl.ds(pl.multiple_of(to_x * QUARTER + to_strip * SLIVER, SLIVER), SLIVER)
            remote(result.at[s, rows, pl.ds(c * W, W)], back[c].at[2 * dp + s], P3 + c, (to, me)).start()
        homes[c, s] = pltpu.make_async_copy(
            result.at[s, my_rows, pl.ds(c * W, W)], back[c].at[2 * dp + s], local_sem.at[4 * CHUNKS + 2 * c + s]
        )
        homes[c, s].start()

    load_right.wait()
    for s in range(2):
        arrive(s).wait_recv()
        for c in range(CHUNKS):
            give_back(s, c)
    for copy in exchanges:
        copy.wait_recv()
    drain += [many(126, P3 + c) for c in range(CHUNKS)]

    load_sl.wait()
    load_sr.wait()

    def gram(i, total, axis):
        s, r, n = i // 4, (i // 2) % 2, i % 2
        rows = pl.ds(pl.multiple_of(r * 256, 256), 256)
        here = pl.ds(pl.multiple_of(me * HALF + r * 256, 256), 256)
        to = pl.ds(pl.multiple_of(n * 512, 512), 512)
        pair = (block[s, here, :], block[s, to, :]) if axis else (block[s, :, here], block[s, :, to])
        product = lax.dot_general(*pair, (((axis,), (axis,)), ((), ())), preferred_element_type=jnp.float32)
        total[s, rows, to] = KEEP * total[s, rows, to] + (1.0 - KEEP) * product

    def gram_left(i, _):
        gram(i, new_left, 1)
        return 0

    def gram_right(i, _):
        gram(i, new_right, 0)
        return 0

    lax.fori_loop(0, 8, gram_left, 0)
    lax.fori_loop(0, 8, gram_right, 0)

    ends = []
    for c in range(CHUNKS):
        many(126, P3 + c).wait_recv()
        for s in range(2):
            homes[c, s].wait()

        def choose(b, _):
            chosen[c, b] = back[c][places[0, b]]
            return 0

        lax.fori_loop(0, BLOCKS, choose, 0, unroll=8)
        rows = pl.ds(pl.multiple_of(strip * SLIVER, SLIVER), SLIVER)
        for offset in plane_order() + [(0, 0, 0)]:
            to, to_strip, _ = chip(offset)
            for core in (me, other):
                for j in range(3):
                    src = chosen.at[c, to_strip * 6 + core * 3 + j]
                    dst = direction.at[rows, pl.ds(pl.multiple_of(j * BS + me * HALF + c * W, 128), W)]
                    if any(offset) or core is other:
                        remote(src, dst, P4 + c, (to, core)).start()
                    else:
                        ends.append(pltpu.make_async_copy(src, dst, local_sem.at[6 * CHUNKS + 3 * c + j]))
                        ends[-1].start()
        drain.append(many(93, P4 + c))
    for c in range(CHUNKS):
        many(93, P4 + c).wait_recv()
    for end in ends:
        end.wait()
    for copy in drain:
        copy.wait_send()


def on_device(grads, slot_block, left_stats, right_stats, left_root, right_root):
    bf16 = jnp.bfloat16
    anywhere = pl.BlockSpec(memory_space=pl.ANY)
    scalars = pl.BlockSpec(memory_space=pltpu.SMEM)
    outs = [(grads.shape, bf16), (left_stats.shape, jnp.float32), (right_stats.shape, jnp.float32)]
    return pl.pallas_call(
        kernel,
        out_shape=[pltpu.VMEM(*out) for out in outs],
        in_specs=[scalars] + [anywhere] * 5,
        out_specs=[pl.BlockSpec(memory_space=pltpu.VMEM)] * 3,
        scratch_shapes=[
            pltpu.VMEM((3, QUARTER, BS), bf16),
            [pltpu.VMEM((BLOCKS + 1, SLIVER, W), bf16) for _ in range(CHUNKS)],
            pltpu.VMEM((CHUNKS, SLOTS, SLIVER, W), bf16),
            pltpu.VMEM((2, BS, BS), bf16),
            pltpu.VMEM((2, BS, BS), bf16),
            pltpu.VMEM((2, BS, HALF), bf16),
            pltpu.VMEM((2, BS, BS), bf16),
            pltpu.VMEM((2, BS, HALF), bf16),
            [pltpu.VMEM((SLOTS, SLIVER, W), bf16) for _ in range(CHUNKS)],
            pltpu.VMEM((CHUNKS, BLOCKS, SLIVER, W), bf16),
            pltpu.VMEM((8, SLOTS), jnp.int32),
            pltpu.SMEM((8, SLOTS), jnp.int32),
            pltpu.SemaphoreType.DMA((8,)),
            pltpu.SemaphoreType.DMA((9 * CHUNKS,)),
            pltpu.SemaphoreType.DMA((3 * CHUNKS + 7,)),
            pltpu.SemaphoreType.DMA((3 * CHUNKS + 7,)),
            pltpu.SemaphoreType.REGULAR,
        ],
        compiler_params=pltpu.CompilerParams(
            collective_id=0, has_side_effects=True, vmem_limit_bytes=50 * 2**20
        ),
    )(slot_block, grads, left_stats, right_stats, left_root, right_root)


def solution(mesh):
    return jax.shard_map(
        on_device,
        mesh=mesh,
        in_specs=(
            P("dp", "mp"),
            P(),
            P("dp", "mp", None),
            P("dp", "mp", None),
            P("dp", "mp", None),
            P("dp", None, "mp"),
        ),
        out_specs=(P("dp", "mp"), P("dp", "mp", None), P("dp", "mp", None)),
        check_vma=False,
    )
```

time: 118 us -> 100 us (0.85)
  Pallas kernels: 105 us -> 94.3 us
  local copies, waits for them, and re-layouts: 9.61 us -> 5.17 us
  other arithmetic: 2.45 us -> 0 us
    pallas_call x1, Pallas kernels: 105 us -> 94.3 us  [on_device(): pl.pallas_call(kernel, out_shape=[pltpu.VMEM(*out) for out in outs], in_s...]
    unnamed x5 -> x3, local copies, waits for them, and re-layouts: 9.61 us -> 5.17 us
    reduce_sum x1 -> x0, other arithmetic: 1.29 us -> none  [on_device(): jnp.sum(jnp.where(matches, jnp.arange(SLOTS, dtype=jnp.int32)[None, :], 0...]
where the time goes in v2:
time: 100 us
  Pallas kernels  94.3 us (94%)
  local copies, waits for them, and re-layouts  5.17 us (5%)
    pallas_call x1, Pallas kernels, on_device(): pl.pallas_call(kernel, out_shape=[pltpu.VMEM(*out) for out in outs], in_s...  94.3 us
    unnamed x3, local copies, waits for them, and re-layouts  5.17 us

profile of v2, /device:TPU:1, one launch (start us, length us, event | category | flops | bytes accessed | tf_op | source)
XLA Modules:
  0.0 100.2 jit_solution(9954723347901970174)
XLA Ops:
  0.6 94.3 %shard_map.85 = (bf16[256,3072]{1,0:T(8,128)(2,1)S(1)}, f32[2,512,1024]{2,1,0:T(8,128)S(1)}, f32[2,512,1024]{2,1,0:T(8,128)S(1)}) custom-call(s32[128]{0:T(128)} %ids.1, bf16[256,3072]{1,0:T(8,128)(2,1)} %grads.1, f32[2,512,1024]{2,1,0:T(8,128)} %left_stats.1, f32[2,512,1024]{2,1,0:T(8,128)} %right_stats.1, bf16[2,512,1024]{2,1,0:T(8,128)(2,1)} %left_root.1, ...), custom_call_target="tpu_custom_call" | custom-call | tf_op jit(solution)/shard_map/pallas_call | solution.py:302
  95.0 1.1 %copy.12 = bf16[256,3072]{1,0:T(8,128)(2,1)} copy(bf16[256,3072]{1,0:T(8,128)(2,1)S(1)} %get-tuple-element.3) | data formatting | bytes 3145728
  96.1 2.0 %copy.13 = f32[2,512,1024]{2,1,0:T(8,128)} copy(f32[2,512,1024]{2,1,0:T(8,128)S(1)} %get-tuple-element.4) | data formatting | bytes 8388608
  98.1 2.0 %copy.14 = f32[2,512,1024]{2,1,0:T(8,128)} copy(f32[2,512,1024]{2,1,0:T(8,128)S(1)} %get-tuple-element.5) | data formatting | bytes 8388608

commit v3 on v2

--- a/solution.py
+++ b/solution.py
@@ -50,18 +50,17 @@
     return order
 
 
-def plane_order():
-    order = []
-    for offset in ((1, 1, 0), (1, 3, 0), (1, 2, 0), (2, 1, 0), (1, 0, 0), (0, 1, 0)):
-        order += [offset, negated(offset)]
-    return order[:4] + [(2, 2, 0)] + order[4:] + [(2, 0, 0), (0, 2, 0)]
+LINES = [(1, 0, 0), (3, 0, 0), (0, 1, 0), (0, 3, 0), (2, 0, 0), (0, 2, 0)]
+DIAGONALS = [
+    (1, 1, 0), (3, 3, 0), (1, 3, 0), (3, 1, 0), (2, 2, 0), (1, 2, 0), (3, 2, 0), (2, 1, 0), (2, 3, 0)
+]
 
 
 def kernel(
-    ids, grads, left_stats, right_stats, left_root, right_root,
+    ids_ref, grads, left_stats, right_stats, left_root, right_root,
     direction, new_left, new_right,
-    window, spread, routed, block, left, right, part, result, back, chosen, table, places,
-    load_sem, local_sem, send_sem, recv_sem, line_sem,
+    window, spread, routed, block, left, right, part, result, back, chosen, table, places, ids,
+    load_sem, local_sem, send_sem, recv_sem, ready_sem,
 ):
     dp, me = lax.axis_index("dp"), lax.axis_index("mp")
     y, z, x = dp // PLANE, (dp // SIDE) % SIDE, dp % SIDE
@@ -88,6 +87,10 @@
         span = routed.at[0, pl.ds(0, pieces)]
         return remote(span, span, sem, (dp, other))
 
+    def slot_copies(s):
+        span = block.at[s, pl.ds(0, 63 * SLIVER), pl.ds(0, HALF)]
+        return remote(span, span, P2 + s, (dp, other))
+
     P1, P3, P4 = 0, CHUNKS, 2 * CHUNKS
     P2, PX, GX, LX = 3 * CHUNKS, 3 * CHUNKS + 2, 3 * CHUNKS + 4, 3 * CHUNKS + 6
 
@@ -98,43 +101,50 @@
     load_right = pltpu.make_async_copy(right_root, right, load_sem.at[4])
     load_sl = pltpu.make_async_copy(left_stats, new_left, load_sem.at[5])
     load_sr = pltpu.make_async_copy(right_stats, new_right, load_sem.at[6])
-    for load in loads:
+    load_ids = pltpu.make_async_copy(ids_ref, ids, load_sem.at[8])
+    for load in loads + [load_ids, load_left, load_right, load_sl, load_sr]:
         load.start()
 
+    def tell(devices, sem):
+        for device in devices:
+            pl.semaphore_signal(sem, inc=1, device_id=device, device_id_type=MESH)
+
+    axes = [[(chip(tuple(n * u for u in unit))[0], me) for n in (1, 2, 3)] for unit in ((1, 0, 0), (0, 1, 0), (0, 0, 1))]
     barrier = pltpu.get_barrier_semaphore()
-    greeted = 0
-    for offset in plane_order():
-        for core in (me, other):
-            pl.semaphore_signal(barrier, inc=1, device_id=(chip(offset)[0], core), device_id_type=MESH)
-            greeted += 1
-    line = [(chip((0, 0, c))[0], me) for c in (1, 2, 3)]
-    for device in [(dp, other)] + line:
-        pl.semaphore_signal(barrier, inc=1, device_id=device, device_id_type=MESH)
-        greeted += 1
-    load_left.start()
-    load_right.start()
-    load_sl.start()
-    load_sr.start()
+    tell(axes[0] + axes[1] + axes[2] + [(dp, other)], barrier)
     for c in range(CHUNKS):
         spread[c][BLOCKS] = jnp.zeros((SLIVER, W), jnp.bfloat16)
-    pl.semaphore_wait(barrier, greeted)
-    for device in line:
-        pl.semaphore_signal(line_sem, inc=1, device_id=device, device_id_type=MESH)
+    pl.semaphore_wait(barrier, 10)
+
+    tell([(dp, other)], ready_sem.at[0])
     for load in loads:
         load.wait()
     mine = pl.ds(strip * 6 + me * 3, 3)
-    kept = []
-    for c in range(CHUNKS):
-        for offset in plane_order() + [(0, 0, 0)]:
+
+    def scatter(offsets, core):
+        for c in range(CHUNKS):
+            for offset in offsets:
+                to, to_strip, _ = chip(offset)
+                rows = pl.ds(pl.multiple_of(to_strip * SLIVER, SLIVER), SLIVER)
+                remote(window.at[:, rows, cols(core, c)], spread[c].at[mine], P1 + c, (to, core)).start()
+
+    scatter(LINES, me)
+    pl.semaphore_wait(ready_sem.at[0], 1)
+    tell(axes[1], ready_sem.at[1])
+    scatter([(0, 0, 0)] + LINES, other)
+    pl.semaphore_wait(ready_sem.at[1], 3)
+    tell(axes[2], ready_sem.at[2])
+    for c in range(CHUNKS):
+        for offset in DIAGONALS:
             to, to_strip, _ = chip(offset)
             rows = pl.ds(pl.multiple_of(to_strip * SLIVER, SLIVER), SLIVER)
             for core in (me, other):
-                src, dst = window.at[:, rows, cols(core, c)], spread[c].at[mine]
-                if any(offset) or core is other:
-                    remote(src, dst, P1 + c, (to, core)).start()
-                else:
-                    kept.append(pltpu.make_async_copy(src, dst, local_sem.at[P1 + c]))
-                    kept[-1].start()
+                remote(window.at[:, rows, cols(core, c)], spread[c].at[mine], P1 + c, (to, core)).start()
+    kept = []
+    for c in range(CHUNKS):
+        rows = pl.ds(pl.multiple_of(strip * SLIVER, SLIVER), SLIVER)
+        kept.append(pltpu.make_async_copy(window.at[:, rows, cols(me, c)], spread[c].at[mine], local_sem.at[P1 + c]))
+        kept[c].start()
         drain.append(many(93, P1 + c))
 
     load_left.wait()
@@ -142,6 +152,7 @@
     send_left.start()
     drain.append(send_left)
 
+    load_ids.wait()
     lanes = lax.broadcasted_iota(jnp.int32, (8, SLOTS), 1)
 
     def seat(slot, seats):
@@ -151,7 +162,7 @@
     fetch = pltpu.make_async_copy(table, places, load_sem.at[7])
     fetch.start()
 
-    pl.semaphore_wait(line_sem, 3)
+    pl.semaphore_wait(ready_sem.at[2], 3)
 
     def pick(c):
         many(93, P1 + c).wait_recv()
@@ -181,13 +192,13 @@
     for c in range(CHUNKS):
         route(c, 1)
     fetch.wait()
-    drain += [many(63 * CHUNKS, P2 + s) for s in range(2)]
+    drain += [slot_copies(s) for s in range(2)]
 
     own = pl.ds(pl.multiple_of(me * HALF, HALF), HALF)
     exchanges = []
 
     def arrive(s):
-        many(63 * CHUNKS, P2 + s).wait_recv()
+        slot_copies(s).wait_recv()
         for c in range(CHUNKS):
             arrivals[c, s].wait()
         send_block = remote(block.at[s, :, own], block.at[s, :, own], GX + s, (dp, other))
@@ -231,19 +242,8 @@
         homes[c, s].start()
 
     load_right.wait()
-    for s in range(2):
-        arrive(s).wait_recv()
-        for c in range(CHUNKS):
-            give_back(s, c)
-    for copy in exchanges:
-        copy.wait_recv()
-    drain += [many(126, P3 + c) for c in range(CHUNKS)]
-
-    load_sl.wait()
-    load_sr.wait()
-
-    def gram(i, total, axis):
-        s, r, n = i // 4, (i // 2) % 2, i % 2
+    def gram(s, i, total, axis):
+        r, n = i // 2, i % 2
         rows = pl.ds(pl.multiple_of(r * 256, 256), 256)
         here = pl.ds(pl.multiple_of(me * HALF + r * 256, 256), 256)
         to = pl.ds(pl.multiple_of(n * 512, 512), 512)
@@ -251,16 +251,24 @@
         product = lax.dot_general(*pair, (((axis,), (axis,)), ((), ())), preferred_element_type=jnp.float32)
         total[s, rows, to] = KEEP * total[s, rows, to] + (1.0 - KEEP) * product
 
-    def gram_left(i, _):
-        gram(i, new_left, 1)
-        return 0
-
-    def gram_right(i, _):
-        gram(i, new_right, 0)
-        return 0
-
-    lax.fori_loop(0, 8, gram_left, 0)
-    lax.fori_loop(0, 8, gram_right, 0)
+    def grams(s):
+        def both(i, _):
+            gram(s, i, new_left, 1)
+            gram(s, i, new_right, 0)
+            return 0
+
+        lax.fori_loop(0, 4, both, 0)
+
+    for s in range(2):
+        arrive(s).wait_recv()
+        for c in range(CHUNKS):
+            give_back(s, c)
+        exchanges[s].wait_recv()
+        if s == 0:
+            load_sl.wait()
+            load_sr.wait()
+        grams(s)
+    drain += [many(126, P3 + c) for c in range(CHUNKS)]
 
     ends = []
     for c in range(CHUNKS):
@@ -274,7 +282,7 @@
 
         lax.fori_loop(0, BLOCKS, choose, 0, unroll=8)
         rows = pl.ds(pl.multiple_of(strip * SLIVER, SLIVER), SLIVER)
-        for offset in plane_order() + [(0, 0, 0)]:
+        for offset in DIAGONALS + LINES + [(0, 0, 0)]:
             to, to_strip, _ = chip(offset)
             for core in (me, other):
                 for j in range(3):
@@ -294,15 +302,23 @@
         copy.wait_send()
 
 
+def write(a, b, c, a_out, b_out, c_out, sem):
+    pairs = [(b, b_out), (c, c_out), (a, a_out)]
+    copies = [pltpu.make_async_copy(src, dst, sem.at[i]) for i, (src, dst) in enumerate(pairs)]
+    for copy in copies:
+        copy.start()
+    for copy in copies:
+        copy.wait()
+
+
 def on_device(grads, slot_block, left_stats, right_stats, left_root, right_root):
     bf16 = jnp.bfloat16
     anywhere = pl.BlockSpec(memory_space=pl.ANY)
-    scalars = pl.BlockSpec(memory_space=pltpu.SMEM)
     outs = [(grads.shape, bf16), (left_stats.shape, jnp.float32), (right_stats.shape, jnp.float32)]
-    return pl.pallas_call(
+    results = pl.pallas_call(
         kernel,
         out_shape=[pltpu.VMEM(*out) for out in outs],
-        in_specs=[scalars] + [anywhere] * 5,
+        in_specs=[anywhere] * 6,
         out_specs=[pl.BlockSpec(memory_space=pltpu.VMEM)] * 3,
         scratch_shapes=[
             pltpu.VMEM((3, QUARTER, BS), bf16),
@@ -317,16 +333,25 @@
             pltpu.VMEM((CHUNKS, BLOCKS, SLIVER, W), bf16),
             pltpu.VMEM((8, SLOTS), jnp.int32),
             pltpu.SMEM((8, SLOTS), jnp.int32),
-            pltpu.SemaphoreType.DMA((8,)),
+            pltpu.SMEM((SLOTS,), jnp.int32),
+            pltpu.SemaphoreType.DMA((9,)),
             pltpu.SemaphoreType.DMA((9 * CHUNKS,)),
             pltpu.SemaphoreType.DMA((3 * CHUNKS + 7,)),
             pltpu.SemaphoreType.DMA((3 * CHUNKS + 7,)),
-            pltpu.SemaphoreType.REGULAR,
+            pltpu.SemaphoreType.REGULAR((3,)),
         ],
         compiler_params=pltpu.CompilerParams(
             collective_id=0, has_side_effects=True, vmem_limit_bytes=50 * 2**20
         ),
     )(slot_block, grads, left_stats, right_stats, left_root, right_root)
+    return pl.pallas_call(
+        write,
+        out_shape=[jax.ShapeDtypeStruct(*out) for out in outs],
+        in_specs=[anywhere] * 3,
+        out_specs=[anywhere] * 3,
+        scratch_shapes=[pltpu.SemaphoreType.DMA((3,))],
+        compiler_params=pltpu.CompilerParams(vmem_limit_bytes=2**20),
+    )(*results)
 
 
 def solution(mesh):

time: 100 us -> 98.1 us (0.981)
  local copies, waits for them, and re-layouts: 5.17 us -> 0 us
  Pallas kernels: 94.3 us -> 97.3 us
    unnamed x3 -> x0, local copies, waits for them, and re-layouts: 5.17 us -> none
    pallas_call x0 -> x1, Pallas kernels: none -> 3.81 us  [on_device(): pl.pallas_call(write, out_shape=[jax.ShapeDtypeStruct(*out) for out in ou...]
where the time goes in v3:
time: 98.1 us; the launch traced here: 97.9 us
  Pallas kernels  97.3 us (99%)
    pallas_call x1, Pallas kernels, on_device(): pl.pallas_call(kernel, out_shape=[pltpu.VMEM(*out) for out in outs], in_s...  93.5 us
    pallas_call x1, Pallas kernels, on_device(): pl.pallas_call(write, out_shape=[jax.ShapeDtypeStruct(*out) for out in ou...  3.81 us

profile of v3, /device:TPU:1, one launch (start us, length us, event | category | flops | bytes accessed | tf_op | source)
XLA Modules:
  0.0 97.9 jit_solution(17762787841248843946)
XLA Ops:
  0.6 93.5 %shard_map.85 = (bf16[256,3072]{1,0:T(8,128)(2,1)S(1)}, f32[2,512,1024]{2,1,0:T(8,128)S(1)}, f32[2,512,1024]{2,1,0:T(8,128)S(1)}) custom-call(s32[128]{0:T(128)} %ids_ref.1, bf16[256,3072]{1,0:T(8,128)(2,1)} %grads.1, f32[2,512,1024]{2,1,0:T(8,128)} %left_stats.1, f32[2,512,1024]{2,1,0:T(8,128)} %right_stats.1, bf16[2,512,1024]{2,1,0:T(8,128)(2,1)} %left_root.1, ...), custom_call_target="tpu_custom_call" | custom-call | tf_op jit(solution)/shard_map/pallas_call | solution.py:318
  94.1 3.8 %shard_map.86 = (bf16[256,3072]{1,0:T(8,128)(2,1)}, f32[2,512,1024]{2,1,0:T(8,128)}, f32[2,512,1024]{2,1,0:T(8,128)}) custom-call(bf16[256,3072]{1,0:T(8,128)(2,1)S(1)} %get-tuple-element.6.a, f32[2,512,1024]{2,1,0:T(8,128)S(1)} %get-tuple-element.7.b, f32[2,512,1024]{2,1,0:T(8,128)S(1)} %get-tuple-element.8.c), custom_call_target="tpu_custom_call" | custom-call | tf_op jit(solution)/shard_map/pallas_call | solution.py:347

commit v4 on v3

--- a/solution.py
+++ b/solution.py
@@ -102,7 +102,7 @@
     load_sl = pltpu.make_async_copy(left_stats, new_left, load_sem.at[5])
     load_sr = pltpu.make_async_copy(right_stats, new_right, load_sem.at[6])
     load_ids = pltpu.make_async_copy(ids_ref, ids, load_sem.at[8])
-    for load in loads + [load_ids, load_left, load_right, load_sl, load_sr]:
+    for load in loads:
         load.start()
 
     def tell(devices, sem):
@@ -129,6 +129,8 @@
                 remote(window.at[:, rows, cols(core, c)], spread[c].at[mine], P1 + c, (to, core)).start()
 
     scatter(LINES, me)
+    for load in (load_ids, load_left, load_right, load_sl, load_sr):
+        load.start()
     pl.semaphore_wait(ready_sem.at[0], 1)
     tell(axes[1], ready_sem.at[1])
     scatter([(0, 0, 0)] + LINES, other)
@@ -147,10 +149,6 @@
         kept[c].start()
         drain.append(many(93, P1 + c))
 
-    load_left.wait()
-    send_left = remote(left.at[:, my_half, :], left.at[:, my_half, :], LX, (dp, other))
-    send_left.start()
-    drain.append(send_left)
 
     load_ids.wait()
     lanes = lax.broadcasted_iota(jnp.int32, (8, SLOTS), 1)
@@ -189,6 +187,11 @@
     for c in range(CHUNKS):
         pick(c)
         route(c, 0)
+        if c == 0:
+            load_left.wait()
+            send_left = remote(left.at[:, my_half, :], left.at[:, my_half, :], LX, (dp, other))
+            send_left.start()
+            drain.append(send_left)
     for c in range(CHUNKS):
         route(c, 1)
     fetch.wait()

time: 98.1 us -> 98.1 us (level)
  no operation moved by 1% of the time
where the time goes in v4:
time: 98.1 us; the launch traced here: 98 us
  Pallas kernels  97.4 us (99%)
    pallas_call x1, Pallas kernels, on_device(): pl.pallas_call(kernel, out_shape=[pltpu.VMEM(*out) for out in outs], in_s...  93.6 us
    pallas_call x1, Pallas kernels, on_device(): pl.pallas_call(write, out_shape=[jax.ShapeDtypeStruct(*out) for out in ou...  3.81 us

profile of v4, /device:TPU:1, one launch (start us, length us, event | category | flops | bytes accessed | tf_op | source)
XLA Modules:
  0.0 98.0 jit_solution(15934225252149559066)
XLA Ops:
  0.6 93.6 %shard_map.85 = (bf16[256,3072]{1,0:T(8,128)(2,1)S(1)}, f32[2,512,1024]{2,1,0:T(8,128)S(1)}, f32[2,512,1024]{2,1,0:T(8,128)S(1)}) custom-call(s32[128]{0:T(128)} %ids_ref.1, bf16[256,3072]{1,0:T(8,128)(2,1)} %grads.1, f32[2,512,1024]{2,1,0:T(8,128)} %left_stats.1, f32[2,512,1024]{2,1,0:T(8,128)} %right_stats.1, bf16[2,512,1024]{2,1,0:T(8,128)(2,1)} %left_root.1, ...), custom_call_target="tpu_custom_call" | custom-call | tf_op jit(solution)/shard_map/pallas_call | solution.py:321
  94.2 3.8 %shard_map.86 = (bf16[256,3072]{1,0:T(8,128)(2,1)}, f32[2,512,1024]{2,1,0:T(8,128)}, f32[2,512,1024]{2,1,0:T(8,128)}) custom-call(bf16[256,3072]{1,0:T(8,128)(2,1)S(1)} %get-tuple-element.6.a, f32[2,512,1024]{2,1,0:T(8,128)S(1)} %get-tuple-element.7.b, f32[2,512,1024]{2,1,0:T(8,128)S(1)} %get-tuple-element.8.c), custom_call_target="tpu_custom_call" | custom-call | tf_op jit(solution)/shard_map/pallas_call | solution.py:350
